TPU v7x, 512 devices: a whole 4x4x16 slice. The times are simulated.
512 devices in a mesh: section: 4 (over y_lo, core), seq: 128 (over z, x, y_hi).
Axes of the slice: x: 4, y: 4 (y_hi: 2, y_lo: 2; y = y_hi * 2 + y_lo), z: 16, core: 2. Of those that a mesh axis runs over, the one named last changes fastest.
Arguments:
- skip_rows: bfloat16 [4, 16384, 2048], P('section', 'seq'), may hold values from -6 to 6
- molecule_kv: bfloat16 [4, 2048, 4096], P('section', 'seq'), may hold values from -139 to 139
- norm_gain: float32 [2048], replicated, may hold values from 0.1 to 1.9
- sink_kv: float32 [2048], replicated, may hold values from -4 to 4
- w_query: bfloat16 [2048, 1024], replicated, may hold values from -0.125 to 0.125
Outputs:
- upsampled: bfloat16 [4, 16384, 1024], P('section', 'seq')
All inputs are finite; a program needn't handle non-finite values.
Results may differ from a plain program's by a relative error of at most 0.014.
The roundings to bfloat16 on the way count: a program that leaves them out, or rounds other values in their place, can miss the bound.
Values may be sent and summed in bfloat16 or wider, within the bound.
No kernel may reach another device: no remote copies, remote signals or barrier semaphores. Data moves between devices by JAX's collectives and lax.ppermute only.
A program may use at most 64 MiB of HBM per device.

v0:
```python
import jax
import jax.numpy as jnp
from jax import lax
from jax.sharding import PartitionSpec as P

NH = 16
HD = 64
SHORT = 4
BACK = 3
HQ = 1024


def passed_along(block, axis, distance):
    devices = range(lax.axis_size(axis))
    route = [((i - distance) % len(devices), i) for i in devices]
    return lax.ppermute(block, axis, route)


def from_behind(value, axis, steps):
    count = lax.axis_size(axis)
    leading, last = (max(0, -steps), min(count, count - steps))
    return lax.ppermute(value, axis, [(source, source + steps) for source in range(leading, last)])


def norm_rows(rows, gain):
    values = rows.astype(jnp.float32)
    inverse = lax.rsqrt(jnp.mean(values * values, axis=-1, keepdims=True) + 1e-06)
    return (values * inverse * gain).astype(jnp.bfloat16)


def attend(query, keyval, sink_kv, block_index, mol_dev):
    chars = query.shape[0]
    width = keyval.shape[1]
    query_heads = query.reshape(chars, NH, HD)
    keys = keyval[:HQ].reshape(NH, HD, width)
    values = keyval[HQ:].reshape(NH, HD, width)
    sink_key = sink_kv[:HQ].reshape(NH, HD)
    sink_value = sink_kv[HQ:].reshape(NH, HD)
    scores = (
        jnp.einsum("qhd,hdk->hqk", query_heads, keys, preferred_element_type=jnp.float32) * 0.125
    )
    sink = jnp.sum(query_heads.astype(jnp.float32) * sink_key[None], axis=-1).T * 0.125
    place = block_index * chars + jnp.arange(chars, dtype=jnp.int32)
    molecule = (block_index - BACK) * mol_dev + jnp.arange(width, dtype=jnp.int32)
    lag = place[:, None] - SHORT * molecule[None, :] - (SHORT - 1)
    visible = (molecule[None, :] >= 0) & (lag >= 0) & (lag < SHORT * BACK * mol_dev)
    scores = jnp.where(visible[None], scores, jnp.float32(-1e30))
    top = jnp.maximum(jnp.max(scores, axis=-1), sink)
    expo = jnp.exp(scores - top[..., None])
    sink_expo = jnp.exp(sink - top)
    total = jnp.sum(expo, axis=-1) + sink_expo
    weight = (expo / total[..., None]).astype(jnp.bfloat16)
    sink_weight = (sink_expo / total).astype(jnp.bfloat16)
    mixed = jnp.einsum("hqk,hdk->qhd", weight, values, preferred_element_type=jnp.float32)
    mixed = mixed + sink_weight.T[..., None].astype(jnp.float32) * sink_value[None]
    return mixed.reshape(chars, HQ).astype(jnp.bfloat16)


def shards(skip_rows, molecule_kv, norm_gain, sink_kv, w_query):
    arrived = passed_along(molecule_kv, "section", 1)
    normed = norm_rows(skip_rows[0], norm_gain)
    query = jnp.dot(normed, w_query, preferred_element_type=jnp.float32).astype(jnp.bfloat16)
    chars = query.shape[0]
    mol_dev = chars // SHORT
    own_block = lax.all_to_all(arrived, "seq", split_axis=2, concat_axis=1, tiled=True)[0]
    pieces = [own_block]
    current = own_block
    for step in range(BACK):
        current = from_behind(current, "seq", 1)
        pieces.insert(0, current)
    keyval = jnp.concatenate(pieces, axis=1)
    block_index = lax.axis_index("seq")
    mixed = attend(query, keyval, sink_kv, block_index, mol_dev)
    return mixed[None]


def solution(mesh):
    return jax.shard_map(
        shards,
        mesh=mesh,
        in_specs=(P("section", "seq", None), P("section", "seq", None), P(), P(), P()),
        out_specs=P("section", "seq", None),
        check_vma=False,
    )
```

profile of v0, /device:TPU:32, one launch (start us, length us, event | category | flops | bytes accessed | tf_op | source)
XLA Modules:
  0.0 130.8 jit_solution(4866062913885767191)
XLA Ops:
  0.0 0.0 copy-start
  0.0 2.0 %collective-permute-start = (bf16[1,16,4096]{2,1,0:T(8,128)(2,1)}, bf16[1,16,4096]{2,1,0:T(8,128)(2,1)S(1)}, u32[]{:S(2)}, u32[]{:S(2)}) collective-permute-start(bf16[1,16,4096]{2,1,0:T(8,128)(2,1)} %param.6), channel_id=1, source_target_pairs={{384,0},{0,128},{128,256},{256,384},{385,1},{1,129},{129,257},{257... | collective-permute-start | bytes 393224 | tf_op jit(solution)/shard_map/ppermute | solution.py:16
  2.1 1.2 fusion.3
  3.3 3.3 %collective-permute-done = bf16[1,16,4096]{2,1,0:T(8,128)(2,1)S(1)} collective-permute-done((bf16[1,16,4096]{2,1,0:T(8,128)(2,1)}, bf16[1,16,4096]{2,1,0:T(8,128)(2,1)S(1)}, u32[]{:S(2)}, u32[]{:S(2)}) %collective-permute-start) | collective-permute-done | bytes 131104 | tf_op jit(solution)/shard_map/ppermute | solution.py:16
  6.6 2.7 %copy.23 = bf16[1,16,4096]{1,0,2:T(2,128)(2,1)S(1)} copy(bf16[1,16,4096]{2,1,0:T(8,128)(2,1)S(1)} %collective-permute-done) | data formatting | bytes 262144 | tf_op jit(solution)/shard_map/ppermute | solution.py:16
  9.3 0.5 broadcast.85
  9.8 22.4 %reduce = bf16[4096,16]{1,0:T(8,128)(2,1)S(1)} reduce(bf16[4096,1,16]{2,1,0:T(2,128)(2,1)S(1)} %bitcast.47, bf16[]{:T(256)} %broadcast.85), dimensions={1}, to_apply=%bitcast.41.reduce_sub_computation | reduce | bytes 262146
  32.2 1.5 %reshape.119 = bf16[128,2,256]{2,1,0:T(2,128)(2,1)} reshape(bf16[4096,16]{1,0:T(8,128)(2,1)S(1)} %reduce) | data formatting | bytes 262144
  33.8 21.6 %all-to-all-start = ((bf16[128,2,256]{2,1,0:T(2,128)(2,1)}), bf16[128,2,256]{2,1,0:T(2,128)(2,1)S(1)}, u32[]{:S(2)}, u32[]{:S(2)}) async-start(bf16[128,2,256]{2,1,0:T(2,128)(2,1)} %reshape.119), calls=%async_computation | async-start | bytes 262144 | tf_op jit(solution)/shard_map/all_to_all | solution.py:65
  55.4 0.0 copy-done
  55.4 3.1 %convolution_convert_fusion = bf16[128,1024]{1,0:T(8,128)(2,1)S(1)} fusion(bf16[2048,1024]{1,0:T(8,128)(2,1)} %param.9, bf16[1,128,2048]{2,1,0:T(8,128)(2,1)} %param.5, f32[2048]{0:T(1024)S(1)} %copy-done, f32[128]{0:T(128)S(1)} %add_rsqrt_fusion), kind=kOutput, calls=%fused_computation.7 | convolution fusion | flops 538050560 | bytes 4989440 | tf_op jit(solution)/shard_map/dot_general | solution.py:62
  58.6 0.0 copy-start.1
  58.6 15.2 %all-to-all-done = bf16[128,2,256]{2,1,0:T(2,128)(2,1)S(1)} async-done(((bf16[128,2,256]{2,1,0:T(2,128)(2,1)}), bf16[128,2,256]{2,1,0:T(2,128)(2,1)S(1)}, u32[]{:S(2)}, u32[]{:S(2)}) %all-to-all-start) | async-done | bytes 131104 | tf_op jit(solution)/shard_map/all_to_all | solution.py:65
  73.8 1.8 %reshape.120 = bf16[4096,1,16]{2,1,0:T(2,128)(2,1)S(1)} reshape(bf16[128,2,256]{2,1,0:T(2,128)(2,1)S(1)} %all-to-all-done) | data formatting | bytes 262144
  75.6 2.0 %copy.24 = bf16[1,16,4096]{2,1,0:T(8,128)(2,1)S(1)} copy(bf16[1,16,4096]{1,0,2:T(2,128)(2,1)S(1)} %bitcast.48) | data formatting | bytes 262144 | tf_op jit(solution)/shard_map/all_to_all | solution.py:65
  77.6 0.4 all_to_all.12
  78.0 0.3 copy.25
  78.3 2.1 %collective-permute-start.1 = (bf16[2048,32]{1,0:T(8,128)(2,1)S(1)}, bf16[2048,32]{1,0:T(8,128)(2,1)S(1)}, u32[]{:S(2)}, u32[]{:S(2)}) collective-permute-start(bf16[2048,32]{1,0:T(8,128)(2,1)S(1)} %bitcast.50), channel_id=1, source_target_pairs={{0,1},{1,2},{2,3},{3,4},{4,5},{5,6},{6,7},{7,8},{8,9},{9,10},{10,1... | collective-permute-start | bytes 393224 | tf_op jit(solution)/shard_map/ppermute | solution.py:22
  80.5 15.4 %collective-permute-done.1 = bf16[2048,32]{1,0:T(8,128)(2,1)S(1)} collective-permute-done((bf16[2048,32]{1,0:T(8,128)(2,1)S(1)}, bf16[2048,32]{1,0:T(8,128)(2,1)S(1)}, u32[]{:S(2)}, u32[]{:S(2)}) %collective-permute-start.1) | collective-permute-done | bytes 131104 | tf_op jit(solution)/shard_map/ppermute | solution.py:22
  95.9 1.9 %collective-permute-start.2 = (bf16[2048,32]{1,0:T(8,128)(2,1)S(1)}, bf16[2048,32]{1,0:T(8,128)(2,1)S(1)}, u32[]{:S(2)}, u32[]{:S(2)}) collective-permute-start(bf16[2048,32]{1,0:T(8,128)(2,1)S(1)} %collective-permute-done.1), channel_id=1, source_target_pairs={{0,1},{1,2},{2,3},{3,4},{4,5},{5,6},{6,7},{7,8},{8,9},{9,10},{10,1... | collective-permute-start | bytes 393224 | tf_op jit(solution)/shard_map/ppermute | solution.py:22
  97.8 0.1 fusion.16
  97.9 14.6 %collective-permute-done.2 = bf16[2048,32]{1,0:T(8,128)(2,1)S(1)} collective-permute-done((bf16[2048,32]{1,0:T(8,128)(2,1)S(1)}, bf16[2048,32]{1,0:T(8,128)(2,1)S(1)}, u32[]{:S(2)}, u32[]{:S(2)}) %collective-permute-start.2) | collective-permute-done | bytes 131104 | tf_op jit(solution)/shard_map/ppermute | solution.py:22
  112.6 1.9 %collective-permute-start.3 = (bf16[2048,32]{1,0:T(8,128)(2,1)S(1)}, bf16[2048,32]{1,0:T(8,128)(2,1)S(1)}, u32[]{:S(2)}, u32[]{:S(2)}) collective-permute-start(bf16[2048,32]{1,0:T(8,128)(2,1)S(1)} %collective-permute-done.2), channel_id=1, source_target_pairs={{0,1},{1,2},{2,3},{3,4},{4,5},{5,6},{6,7},{7,8},{8,9},{9,10},{10,1... | collective-permute-start | bytes 393224 | tf_op jit(solution)/shard_map/ppermute | solution.py:22
  114.5 0.0 copy-done.1
  114.5 0.2 copy.26
  114.7 0.1 mul.88
  114.8 0.1 mul.95
  114.8 0.2 multiply_reduce_fusion
  115.0 13.2 %collective-permute-done.3 = bf16[2048,32]{1,0:T(8,128)(2,1)S(1)} collective-permute-done((bf16[2048,32]{1,0:T(8,128)(2,1)S(1)}, bf16[2048,32]{1,0:T(8,128)(2,1)S(1)}, u32[]{:S(2)}, u32[]{:S(2)}) %collective-permute-start.3) | collective-permute-done | bytes 131104 | tf_op jit(solution)/shard_map/ppermute | solution.py:22
  128.3 0.7 pad_maximum_fusion
  129.0 0.4 fusion.26
  129.4 0.2 fusion.6
  129.6 0.3 fusion.2
  129.9 0.9 copy.28
  (8 shorter events, 0.1 us)
Async XLA Ops:
  0.0 55.4 %copy-start = (f32[2048]{0:T(1024)S(1)}, f32[2048]{0:T(1024)}, u32[]{:S(2)}) copy-start(f32[2048]{0:T(1024)} %param.7) | copy-start | bytes 24580
  0.0 6.6 %collective-permute-start = (bf16[1,16,4096]{2,1,0:T(8,128)(2,1)}, bf16[1,16,4096]{2,1,0:T(8,128)(2,1)S(1)}, u32[]{:S(2)}, u32[]{:S(2)}) collective-permute-start(bf16[1,16,4096]{2,1,0:T(8,128)(2,1)} %param.6), channel_id=1, source_target_pairs={{384,0},{0,128},{128,256},{256,384},{385,1},{1,129},{129,257},{257... | collective-permute-start | bytes 393224 | tf_op jit(solution)/shard_map/ppermute | solution.py:16
  33.8 40.0 %all-to-all-start = ((bf16[128,2,256]{2,1,0:T(2,128)(2,1)}), bf16[128,2,256]{2,1,0:T(2,128)(2,1)S(1)}, u32[]{:S(2)}, u32[]{:S(2)}) async-start(bf16[128,2,256]{2,1,0:T(2,128)(2,1)} %reshape.119), calls=%async_computation | async-start | bytes 262144 | tf_op jit(solution)/shard_map/all_to_all | solution.py:65
  58.6 55.9 %copy-start.1 = (f32[2048]{0:T(1024)S(1)}, f32[2048]{0:T(1024)}, u32[]{:S(2)}) copy-start(f32[2048]{0:T(1024)} %param.8) | copy-start | bytes 24580
  78.3 17.6 %collective-permute-start.1 = (bf16[2048,32]{1,0:T(8,128)(2,1)S(1)}, bf16[2048,32]{1,0:T(8,128)(2,1)S(1)}, u32[]{:S(2)}, u32[]{:S(2)}) collective-permute-start(bf16[2048,32]{1,0:T(8,128)(2,1)S(1)} %bitcast.50), channel_id=1, source_target_pairs={{0,1},{1,2},{2,3},{3,4},{4,5},{5,6},{6,7},{7,8},{8,9},{9,10},{10,1... | collective-permute-start | bytes 393224 | tf_op jit(solution)/shard_map/ppermute | solution.py:22
  95.9 16.6 %collective-permute-start.2 = (bf16[2048,32]{1,0:T(8,128)(2,1)S(1)}, bf16[2048,32]{1,0:T(8,128)(2,1)S(1)}, u32[]{:S(2)}, u32[]{:S(2)}) collective-permute-start(bf16[2048,32]{1,0:T(8,128)(2,1)S(1)} %collective-permute-done.1), channel_id=1, source_target_pairs={{0,1},{1,2},{2,3},{3,4},{4,5},{5,6},{6,7},{7,8},{8,9},{9,10},{10,1... | collective-permute-start | bytes 393224 | tf_op jit(solution)/shard_map/ppermute | solution.py:22
  112.6 15.7 %collective-permute-start.3 = (bf16[2048,32]{1,0:T(8,128)(2,1)S(1)}, bf16[2048,32]{1,0:T(8,128)(2,1)S(1)}, u32[]{:S(2)}, u32[]{:S(2)}) collective-permute-start(bf16[2048,32]{1,0:T(8,128)(2,1)S(1)} %collective-permute-done.2), channel_id=1, source_target_pairs={{0,1},{1,2},{2,3},{3,4},{4,5},{5,6},{6,7},{7,8},{8,9},{9,10},{10,1... | collective-permute-start | bytes 393224 | tf_op jit(solution)/shard_map/ppermute | solution.py:22
where the time goes:
time: 131 us
  waiting for transfers between devices  61.9 us (47%)
  starting transfers between devices  29.6 us (23%)
  other arithmetic  24.9 us (19%)
  local copies, waits for them, and re-layouts  10.4 us (8%)
  matrix products  3.8 us (3%)
    ppermute x3, waiting for transfers between devices, from_behind(): lax.ppermute(value, axis, [(source, source + steps) for source in range(l...  43.3 us
    unnamed x1, other arithmetic  22.4 us
    all_to_all x1, starting transfers between devices, shards(): lax.all_to_all(arrived, 'seq', split_axis=2, concat_axis=1, tiled=True)[0]  21.6 us
    all_to_all x1, waiting for transfers between devices, shards(): lax.all_to_all(arrived, 'seq', split_axis=2, concat_axis=1, tiled=True)[0]  15.2 us
    ppermute x3, starting transfers between devices, from_behind(): lax.ppermute(value, axis, [(source, source + steps) for source in range(l...  5.96 us
    unnamed x7, local copies, waits for them, and re-layouts  3.87 us
    ppermute x1, waiting for transfers between devices, passed_along(): return lax.ppermute(block, axis, route)  3.33 us
    dot_general x1, matrix products, shards(): jnp.dot(normed, w_query, preferred_element_type=jnp.float32)  3.12 us
  transfers between devices with their start and end apart: 5, of which 5 were waited for; matrix products, arithmetic and copies ran while one was open for 4% of the time, Pallas kernels for 0%

commit v1 on v0

v1 whole, which is shorter than its diff:
```python
import functools

import jax
import jax.numpy as jnp
from jax import lax
from jax.experimental import pallas as pl
from jax.experimental.pallas import tpu as pltpu
from jax.sharding import PartitionSpec as P

NH = 16
HD = 64
SHORT = 4
BACK = 3
HQ = 1024
LANES = 128
PLANE = 8
ROWS = 16
VMEM = pl.BlockSpec(memory_space=pltpu.VMEM)
SMALL = pltpu.CompilerParams(vmem_limit_bytes=16 * 1024 * 1024)


def norm_rows(rows, gain):
    values = rows.astype(jnp.float32)
    inverse = lax.rsqrt(jnp.mean(values * values, axis=-1, keepdims=True) + 1e-06)
    return (values * inverse * gain).astype(jnp.bfloat16)


def spread_kernel(kv_ref, out_ref):
    planes, _, wide = out_ref.shape
    step = kv_ref.shape[1] // planes
    for c in range(planes):
        first = c * step - (wide - step)
        if first < 0:
            out_ref[c, :, : wide - step] = jnp.zeros((ROWS, wide - step), jnp.bfloat16)
            out_ref[c, :, wide - step :] = kv_ref[:, :step]
        else:
            out_ref[c] = kv_ref[:, first : first + wide]


def window_kernel(in_ref, out_ref):
    rows = in_ref.shape[0] * in_ref.shape[1]
    data = in_ref[...].reshape(rows, in_ref.shape[2])
    for w in range(PLANE):
        first = 32 * w + 32
        out_ref[w] = data[:, first : first + LANES]


def attend_kernel(q_ref, kv_ref, sink_ref, value_ref, out_ref):
    chars = q_ref.shape[0]
    block = lax.axis_index("seq")
    char = lax.broadcasted_iota(jnp.int32, (chars, 2 * LANES), 0)
    slot = lax.rem(lax.broadcasted_iota(jnp.int32, (chars, 2 * LANES), 1), LANES)
    lag = char - SHORT * slot + (SHORT * BACK * 32 - (SHORT - 1))
    visible = (lag >= 0) & (lag < SHORT * BACK * 32) & (slot >= (BACK - block) * 32)
    zero = jnp.zeros((HD, LANES), jnp.bfloat16)
    left = lax.broadcasted_iota(jnp.int32, (chars, LANES), 1) < HD

    def pair(first):
        parts = [kv_ref[w, first : first + ROWS, :] for w in range(PLANE)]
        even = jnp.concatenate(parts[: PLANE // 2], axis=0)
        odd = jnp.concatenate(parts[PLANE // 2 :], axis=0)
        return jnp.concatenate(
            [jnp.concatenate([even, zero], axis=1), jnp.concatenate([zero, odd], axis=1)], axis=0
        )

    for m in range(NH // 2):
        lanes = slice(m * LANES, (m + 1) * LANES)
        scores = jnp.dot(q_ref[:, lanes], pair(m * ROWS), preferred_element_type=jnp.float32)
        scores = jnp.where(visible, scores * 0.125, jnp.float32(-1e30))
        weights, sinks = [], []
        for side in range(2):
            score = scores[:, side * LANES : (side + 1) * LANES]
            sink = sink_ref[:, 2 * m + side : 2 * m + side + 1]
            top = jnp.maximum(jnp.max(score, axis=-1, keepdims=True), sink)
            expo = jnp.exp(score - top)
            sink_expo = jnp.exp(sink - top)
            total = jnp.sum(expo, axis=-1, keepdims=True) + sink_expo
            weights.append((expo / total).astype(jnp.bfloat16))
            sinks.append((sink_expo / total).astype(jnp.bfloat16).astype(jnp.float32))
        mixed = lax.dot_general(
            jnp.concatenate(weights, axis=1),
            pair((m + NH // 2) * ROWS),
            (((1,), (1,)), ((), ())),
            preferred_element_type=jnp.float32,
        )
        mixed = mixed + jnp.where(left, sinks[0], sinks[1]) * value_ref[:, lanes]
        out_ref[:, lanes] = mixed.astype(jnp.bfloat16)


def shards(skip_rows, molecule_kv, norm_gain, sink_kv, w_query):
    seq = lax.axis_size("seq")
    sections = lax.axis_size("section")
    planes = seq // PLANE
    columns = [[z * PLANE + w for z in range(planes)] for w in range(PLANE)]
    rows = [[z * PLANE + w for w in range(PLANE)] for z in range(planes)]
    width = molecule_kv.shape[2] // planes

    arrived = lax.ppermute(
        molecule_kv, "section", [((i - 1) % sections, i) for i in range(sections)]
    )[0]
    normed = norm_rows(skip_rows[0], norm_gain)
    query = jnp.dot(normed, w_query, preferred_element_type=jnp.float32).astype(jnp.bfloat16)
    chars = query.shape[0]
    sink_key = sink_kv[:HQ].reshape(NH, HD)
    sink = jnp.sum(query.astype(jnp.float32).reshape(chars, NH, HD) * sink_key[None], axis=-1)
    sink = sink * 0.125

    chunks = pl.pallas_call(
        spread_kernel,
        out_shape=jax.ShapeDtypeStruct((planes, ROWS, width + LANES), jnp.bfloat16),
        in_specs=[VMEM],
        out_specs=VMEM,
        compiler_params=SMALL,
    )(arrived)
    chunks = lax.all_to_all(chunks, "seq", 0, 0, axis_index_groups=columns, tiled=True)
    windows = pl.pallas_call(
        window_kernel,
        out_shape=jax.ShapeDtypeStruct((PLANE, planes * ROWS, LANES), jnp.bfloat16),
        in_specs=[VMEM],
        out_specs=VMEM,
        compiler_params=SMALL,
    )(chunks)
    keyval = lax.all_to_all(windows, "seq", 0, 0, axis_index_groups=rows, tiled=True)
    mixed = pl.pallas_call(
        attend_kernel,
        out_shape=jax.ShapeDtypeStruct((chars, HQ), jnp.bfloat16),
        in_specs=[VMEM] * 4,
        out_specs=VMEM,
        compiler_params=SMALL,
    )(query, keyval, sink, sink_kv[HQ:][None])
    return mixed[None]


def solution(mesh):
    return jax.shard_map(
        shards,
        mesh=mesh,
        in_specs=(P("section", "seq", None), P("section", "seq", None), P(), P(), P()),
        out_specs=P("section", "seq", None),
        check_vma=False,
    )
```

time: 131 us -> 61.5 us (0.47)
  waiting for transfers between devices: 61.9 us -> 25 us
  other arithmetic: 24.9 us -> 1.45 us
  local copies, waits for them, and re-layouts: 10.4 us -> 0.31 us
  Pallas kernels: 0 us -> 6.8 us
  starting transfers between devices: 29.6 us -> 24.3 us
    ppermute x4 -> x1, waiting for transfers between devices: 46.6 us -> 4.57 us  [shards(): lax.ppermute(molecule_kv, 'section', [((i - 1) % sections, i) for i in ra...]
    unnamed x1 -> x0, other arithmetic: 22.4 us -> none
    pallas_call x0 -> x3, Pallas kernels: none -> 6.8 us  [the longest x1 5.06 us: shards(): pl.pallas_call(attend_kernel, out_shape=jax.ShapeDtypeStruct((chars, HQ),...]
    ppermute x4 -> x1, starting transfers between devices: 8 us -> 2.04 us  [shards(): lax.ppermute(molecule_kv, 'section', [((i - 1) % sections, i) for i in ra...]
    all_to_all x1 -> x2, waiting for transfers between devices: 15.2 us -> 20.4 us  [the longest x1 11.3 us: shards(): lax.all_to_all(chunks, 'seq', 0, 0, axis_index_groups=columns, tiled=True)]
    unnamed x7 -> x2, local copies, waits for them, and re-layouts: 3.87 us -> 0.01 us
    all_to_all x3 -> x0, local copies, waits for them, and re-layouts: 2.7 us -> none  [shards(): lax.all_to_all(arrived, 'seq', split_axis=2, concat_axis=1, tiled=True)[0]]
    ppermute x1 -> x0, local copies, waits for them, and re-layouts: 2.66 us -> none  [passed_along(): return lax.ppermute(block, axis, route)]
  transfers between devices with their start and end apart: 5 -> 3, of which waited for: 5 -> 3; matrix products, arithmetic and copies ran while one was open for 4% -> 8% of each run, Pallas kernels for 0% -> 0%
where the time goes in v1:
time: 61.5 us; the launch traced here: 61.1 us
  waiting for transfers between devices  25 us (41%)
  starting transfers between devices  24.3 us (40%)
  Pallas kernels  6.8 us (11%)
  matrix products  3.13 us (5%)
  other arithmetic  1.45 us (2%)
    all_to_all x1, starting transfers between devices, shards(): lax.all_to_all(chunks, 'seq', 0, 0, axis_index_groups=columns, tiled=True)  15.2 us
    all_to_all x1, waiting for transfers between devices, shards(): lax.all_to_all(chunks, 'seq', 0, 0, axis_index_groups=columns, tiled=True)  11.3 us
    all_to_all x1, waiting for transfers between devices, shards(): lax.all_to_all(windows, 'seq', 0, 0, axis_index_groups=rows, tiled=True)  9.13 us
    all_to_all x1, starting transfers between devices, shards(): lax.all_to_all(windows, 'seq', 0, 0, axis_index_groups=rows, tiled=True)  7.09 us
    pallas_call x1, Pallas kernels, shards(): pl.pallas_call(attend_kernel, out_shape=jax.ShapeDtypeStruct((chars, HQ),...  5.06 us
    ppermute x1, waiting for transfers between devices, shards(): lax.ppermute(molecule_kv, 'section', [((i - 1) % sections, i) for i in ra...  4.57 us
    dot_general x1, matrix products, shards(): jnp.dot(normed, w_query, preferred_element_type=jnp.float32)  3.13 us
    ppermute x1, starting transfers between devices, shards(): lax.ppermute(molecule_kv, 'section', [((i - 1) % sections, i) for i in ra...  2.04 us
  transfers between devices with their start and end apart: 3, of which 3 were waited for; matrix products, arithmetic and copies ran while one was open for 8% of the time, Pallas kernels for 0%

profile of v1, /device:TPU:32, one launch (start us, length us, event | category | flops | bytes accessed | tf_op | source)
XLA Modules:
  0.0 61.1 jit_solution(2929294442254292207)
XLA Ops:
  0.0 0.0 copy-start
  0.0 2.0 %collective-permute-start = (bf16[1,16,4096]{2,1,0:T(8,128)(2,1)}, bf16[1,16,4096]{2,1,0:T(8,128)(2,1)S(1)}, u32[]{:S(2)}, u32[]{:S(2)}) collective-permute-start(bf16[1,16,4096]{2,1,0:T(8,128)(2,1)} %param.6), channel_id=1, source_target_pairs={{384,0},{0,128},{128,256},{256,384},{385,1},{1,129},{129,257},{257... | collective-permute-start | bytes 393224 | tf_op jit(solution)/shard_map/ppermute | solution.py:98
  2.0 4.6 %collective-permute-done = bf16[1,16,4096]{2,1,0:T(8,128)(2,1)S(1)} collective-permute-done((bf16[1,16,4096]{2,1,0:T(8,128)(2,1)}, bf16[1,16,4096]{2,1,0:T(8,128)(2,1)S(1)}, u32[]{:S(2)}, u32[]{:S(2)}) %collective-permute-start) | collective-permute-done | bytes 131104 | tf_op jit(solution)/shard_map/ppermute | solution.py:98
  6.6 0.7 %shard_map.55 = bf16[16,16,384]{2,1,0:T(8,128)(2,1)} custom-call(bf16[16,4096]{1,0:T(8,128)(2,1)S(1)} %bitcast.13), custom_call_target="tpu_custom_call" | custom-call | tf_op jit(solution)/shard_map/pallas_call | solution.py:108
  7.3 15.2 %all-to-all-start = ((bf16[16,16,384]{2,1,0:T(8,128)(2,1)}), bf16[16,16,384]{2,1,0:T(8,128)(2,1)S(1)}, u32[]{:S(2)}, u32[]{:S(2)}) async-start(bf16[16,16,384]{2,1,0:T(8,128)(2,1)} %shard_map.55), calls=%async_computation | async-start | bytes 393216 | tf_op jit(solution)/shard_map/all_to_all | solution.py:115
  22.5 1.2 %fusion = f32[128]{0:T(128)S(1)} fusion(bf16[1,128,2048]{2,1,0:T(8,128)(2,1)} %param.5), kind=kLoop, calls=%fused_computation.3 | loop fusion | flops 786304 | bytes 524800 | tf_op jit(solution)/shard_map/reduce_sum | solution.py:24
  23.8 3.1 %convolution_convert_fusion.q_ref = bf16[128,1024]{1,0:T(8,128)(2,1)S(1)} fusion(bf16[2048,1024]{1,0:T(8,128)(2,1)} %param.9, bf16[1,128,2048]{2,1,0:T(8,128)(2,1)} %param.5, f32[2048]{0:T(1024)} %param.7, f32[128]{0:T(128)S(1)} %add_rsqrt_fusion), kind=kOutput, calls=%fused_computation.2 | convolution fusion | flops 538050560 | bytes 4989440 | tf_op jit(solution)/shard_map/dot_general | solution.py:102
  26.9 11.3 %all-to-all-done.in_ref = bf16[16,16,384]{2,1,0:T(8,128)(2,1)S(1)} async-done(((bf16[16,16,384]{2,1,0:T(8,128)(2,1)}), bf16[16,16,384]{2,1,0:T(8,128)(2,1)S(1)}, u32[]{:S(2)}, u32[]{:S(2)}) %all-to-all-start) | async-done | bytes 196640 | tf_op jit(solution)/shard_map/all_to_all | solution.py:115
  38.2 1.1 %shard_map.56 = bf16[8,256,128]{2,1,0:T(8,128)(2,1)} custom-call(bf16[16,16,384]{2,1,0:T(8,128)(2,1)S(1)} %all-to-all-done.in_ref), custom_call_target="tpu_custom_call" | custom-call | tf_op jit(solution)/shard_map/pallas_call | solution.py:116
  39.3 7.1 %all-to-all-start.1 = ((bf16[8,256,128]{2,1,0:T(8,128)(2,1)}), bf16[8,256,128]{2,1,0:T(8,128)(2,1)S(1)}, u32[]{:S(2)}, u32[]{:S(2)}) async-start(bf16[8,256,128]{2,1,0:T(8,128)(2,1)} %shard_map.56), calls=%async_computation.1 | async-start | bytes 1048576 | tf_op jit(solution)/shard_map/all_to_all | solution.py:123
  46.3 0.0 copy-done
  46.4 0.1 mul.40
  46.4 0.1 copy.9
  46.6 0.2 multiply_reduce_fusion
  46.8 0.1 copy.10
  46.9 9.1 %all-to-all-done.1.kv_ref = bf16[8,256,128]{2,1,0:T(8,128)(2,1)S(1)} async-done(((bf16[8,256,128]{2,1,0:T(8,128)(2,1)}), bf16[8,256,128]{2,1,0:T(8,128)(2,1)S(1)}, u32[]{:S(2)}, u32[]{:S(2)}) %all-to-all-start.1) | async-done | bytes 524320 | tf_op jit(solution)/shard_map/all_to_all | solution.py:123
  56.0 5.1 %shard_map.57 = bf16[128,1024]{1,0:T(8,128)(2,1)} custom-call(bf16[128,1024]{1,0:T(8,128)(2,1)S(1)} %convolution_convert_fusion.q_ref, bf16[8,256,128]{2,1,0:T(8,128)(2,1)S(1)} %all-to-all-done.1.kv_ref, f32[128,16]{1,0:T(8,128)S(1)} %broadcast_multiply_fusion.sink_ref, f32[1,1024]{1,0:T(1,128)S(1)} %bitcast.14), custom_call_target="tpu_custom_call" | custom-call | tf_op jit(solution)/shard_map/pallas_call | solution.py:124
  (3 shorter events, 0.0 us)
Async XLA Ops:
  0.0 46.3 %copy-start = (f32[2048]{0:T(1024)S(1)}, f32[2048]{0:T(1024)}, u32[]{:S(2)}) copy-start(f32[2048]{0:T(1024)} %param.8) | copy-start | bytes 24580
  0.0 6.6 %collective-permute-start = (bf16[1,16,4096]{2,1,0:T(8,128)(2,1)}, bf16[1,16,4096]{2,1,0:T(8,128)(2,1)S(1)}, u32[]{:S(2)}, u32[]{:S(2)}) collective-permute-start(bf16[1,16,4096]{2,1,0:T(8,128)(2,1)} %param.6), channel_id=1, source_target_pairs={{384,0},{0,128},{128,256},{256,384},{385,1},{1,129},{129,257},{257... | collective-permute-start | bytes 393224 | tf_op jit(solution)/shard_map/ppermute | solution.py:98
  7.3 30.9 %all-to-all-start = ((bf16[16,16,384]{2,1,0:T(8,128)(2,1)}), bf16[16,16,384]{2,1,0:T(8,128)(2,1)S(1)}, u32[]{:S(2)}, u32[]{:S(2)}) async-start(bf16[16,16,384]{2,1,0:T(8,128)(2,1)} %shard_map.55), calls=%async_computation | async-start | bytes 393216 | tf_op jit(solution)/shard_map/all_to_all | solution.py:115
  39.3 16.8 %all-to-all-start.1 = ((bf16[8,256,128]{2,1,0:T(8,128)(2,1)}), bf16[8,256,128]{2,1,0:T(8,128)(2,1)S(1)}, u32[]{:S(2)}, u32[]{:S(2)}) async-start(bf16[8,256,128]{2,1,0:T(8,128)(2,1)} %shard_map.56), calls=%async_computation.1 | async-start | bytes 1048576 | tf_op jit(solution)/shard_map/all_to_all | solution.py:123

commit v2 on v1

--- a/solution.py
+++ b/solution.py
@@ -46,45 +46,51 @@
 
 
 def attend_kernel(q_ref, kv_ref, sink_ref, value_ref, out_ref):
-    chars = q_ref.shape[0]
+    chars = q_ref.shape[1]
     block = lax.axis_index("seq")
-    char = lax.broadcasted_iota(jnp.int32, (chars, 2 * LANES), 0)
-    slot = lax.rem(lax.broadcasted_iota(jnp.int32, (chars, 2 * LANES), 1), LANES)
+    char = lax.broadcasted_iota(jnp.int32, (LANES, chars), 1)
+    slot = lax.broadcasted_iota(jnp.int32, (LANES, chars), 0)
     lag = char - SHORT * slot + (SHORT * BACK * 32 - (SHORT - 1))
     visible = (lag >= 0) & (lag < SHORT * BACK * 32) & (slot >= (BACK - block) * 32)
-    zero = jnp.zeros((HD, LANES), jnp.bfloat16)
-    left = lax.broadcasted_iota(jnp.int32, (chars, LANES), 1) < HD
+    hidden = jnp.where(visible, jnp.float32(0.0), jnp.float32(-1e30))
+    zero = jnp.zeros((HD, chars), jnp.bfloat16)
 
     def pair(first):
-        parts = [kv_ref[w, first : first + ROWS, :] for w in range(PLANE)]
-        even = jnp.concatenate(parts[: PLANE // 2], axis=0)
-        odd = jnp.concatenate(parts[PLANE // 2 :], axis=0)
-        return jnp.concatenate(
-            [jnp.concatenate([even, zero], axis=1), jnp.concatenate([zero, odd], axis=1)], axis=0
-        )
+        return jnp.concatenate([kv_ref[w, first : first + ROWS, :] for w in range(PLANE)], axis=0)
 
     for m in range(NH // 2):
-        lanes = slice(m * LANES, (m + 1) * LANES)
-        scores = jnp.dot(q_ref[:, lanes], pair(m * ROWS), preferred_element_type=jnp.float32)
-        scores = jnp.where(visible, scores * 0.125, jnp.float32(-1e30))
+        rows = slice(m * LANES, (m + 1) * LANES)
+        query = q_ref[rows, :]
+        query = jnp.concatenate(
+            [
+                jnp.concatenate([query[:HD], zero], axis=0),
+                jnp.concatenate([zero, query[HD:]], axis=0),
+            ],
+            axis=1,
+        )
+        scores = lax.dot_general(
+            pair(m * ROWS), query, (((0,), (0,)), ((), ())), preferred_element_type=jnp.float32
+        )
         weights, sinks = [], []
         for side in range(2):
-            score = scores[:, side * LANES : (side + 1) * LANES]
-            sink = sink_ref[:, 2 * m + side : 2 * m + side + 1]
-            top = jnp.maximum(jnp.max(score, axis=-1, keepdims=True), sink)
+            score = scores[:, side * chars : (side + 1) * chars] * 0.125 + hidden
+            sink = sink_ref[2 * m + side : 2 * m + side + 1, :]
+            top = jnp.maximum(jnp.max(score, axis=0, keepdims=True), sink)
             expo = jnp.exp(score - top)
             sink_expo = jnp.exp(sink - top)
-            total = jnp.sum(expo, axis=-1, keepdims=True) + sink_expo
-            weights.append((expo / total).astype(jnp.bfloat16))
-            sinks.append((sink_expo / total).astype(jnp.bfloat16).astype(jnp.float32))
-        mixed = lax.dot_general(
+            inverse = 1.0 / (jnp.sum(expo, axis=0, keepdims=True) + sink_expo)
+            weights.append((expo * inverse).astype(jnp.bfloat16))
+            sinks.append((sink_expo * inverse).astype(jnp.bfloat16).astype(jnp.float32))
+        mixed = jnp.dot(
+            pair((m + NH // 2) * ROWS),
             jnp.concatenate(weights, axis=1),
-            pair((m + NH // 2) * ROWS),
-            (((1,), (1,)), ((), ())),
             preferred_element_type=jnp.float32,
         )
-        mixed = mixed + jnp.where(left, sinks[0], sinks[1]) * value_ref[:, lanes]
-        out_ref[:, lanes] = mixed.astype(jnp.bfloat16)
+        value = value_ref[rows, :]
+        even = mixed[:HD, :chars] + sinks[0] * value[:HD]
+        odd = mixed[HD:, chars:] + sinks[1] * value[HD:]
+        mixed = jnp.concatenate([even, odd], axis=0)
+        out_ref[:, rows] = mixed.T.astype(jnp.bfloat16)
 
 
 def shards(skip_rows, molecule_kv, norm_gain, sink_kv, w_query):
@@ -101,9 +107,10 @@
     normed = norm_rows(skip_rows[0], norm_gain)
     query = jnp.dot(normed, w_query, preferred_element_type=jnp.float32).astype(jnp.bfloat16)
     chars = query.shape[0]
-    sink_key = sink_kv[:HQ].reshape(NH, HD)
-    sink = jnp.sum(query.astype(jnp.float32).reshape(chars, NH, HD) * sink_key[None], axis=-1)
-    sink = sink * 0.125
+    turned = query.T
+    sink = turned.astype(jnp.float32).reshape(NH, HD, chars) * sink_kv[:HQ].reshape(NH, HD, 1)
+    sink = jnp.sum(sink, axis=1) * 0.125
+    sink_value = jnp.broadcast_to(sink_kv[HQ:, None], (HQ, chars))
 
     chunks = pl.pallas_call(
         spread_kernel,
@@ -113,6 +120,7 @@
         compiler_params=SMALL,
     )(arrived)
     chunks = lax.all_to_all(chunks, "seq", 0, 0, axis_index_groups=columns, tiled=True)
+    chunks, turned, sink, sink_value = lax.optimization_barrier((chunks, turned, sink, sink_value))
     windows = pl.pallas_call(
         window_kernel,
         out_shape=jax.ShapeDtypeStruct((PLANE, planes * ROWS, LANES), jnp.bfloat16),
@@ -127,7 +135,7 @@
         in_specs=[VMEM] * 4,
         out_specs=VMEM,
         compiler_params=SMALL,
-    )(query, keyval, sink, sink_kv[HQ:][None])
+    )(turned, keyval, sink, sink_value)
     return mixed[None]
 
 

time: 61.5 us -> 57.1 us (0.928)
  blocking collectives: 0 us -> 16.7 us
  waiting for transfers between devices: 25 us -> 14 us
  starting transfers between devices: 24.3 us -> 17.1 us
  Pallas kernels: 6.8 us -> 2.48 us
  matrix products: 3.13 us -> 4.22 us
  local copies, waits for them, and re-layouts: 0.31 us -> 0.96 us
    all_to_all x0 -> x1, blocking collectives: none -> 16.7 us  [shards(): lax.all_to_all(windows, 'seq', 0, 0, axis_index_groups=rows, tiled=True)]
    all_to_all x1 -> x0, waiting for transfers between devices: 9.13 us -> none  [shards(): lax.all_to_all(windows, 'seq', 0, 0, axis_index_groups=rows, tiled=True)]
    all_to_all x1 -> x0, starting transfers between devices: 7.09 us -> none  [shards(): lax.all_to_all(windows, 'seq', 0, 0, axis_index_groups=rows, tiled=True)]
    pallas_call x1, Pallas kernels: 5.06 us -> 1.51 us  [shards(): pl.pallas_call(attend_kernel, out_shape=jax.ShapeDtypeStruct((chars, HQ),...]
    all_to_all x1, waiting for transfers between devices: 11.3 us -> 9.43 us  [shards(): lax.all_to_all(chunks, 'seq', 0, 0, axis_index_groups=columns, tiled=True)]
    dot_general x1, matrix products: 3.13 us -> 4.22 us  [shards(): jnp.dot(normed, w_query, preferred_element_type=jnp.float32)]
    pallas_call x1, Pallas kernels: 1.05 us -> 0.27 us  [shards(): pl.pallas_call(window_kernel, out_shape=jax.ShapeDtypeStruct((PLANE, plan...]
    slice x1, local copies, waits for them, and re-layouts: 0.01 us -> 0.7 us  [shards(): sink_value = jnp.broadcast_to(sink_kv[HQ:, None], (HQ, chars))]
  transfers between devices with their start and end apart: 3 -> 2, of which waited for: 3 -> 2; matrix products, arithmetic and copies ran while one was open for 8% -> 11% of each run, Pallas kernels for 0% -> 0%
where the time goes in v2:
time: 57.1 us; the launch traced here: 56.8 us
  starting transfers between devices  17.1 us (30%)
  blocking collectives  16.7 us (29%)
  waiting for transfers between devices  14 us (25%)
  matrix products  4.22 us (7%)
  Pallas kernels  2.48 us (4%)
  other arithmetic  1.24 us (2%)
  local copies, waits for them, and re-layouts  0.96 us (2%)
    all_to_all x1, blocking collectives, shards(): lax.all_to_all(windows, 'seq', 0, 0, axis_index_groups=rows, tiled=True)  16.7 us
    all_to_all x1, starting transfers between devices, shards(): lax.all_to_all(chunks, 'seq', 0, 0, axis_index_groups=columns, tiled=True)  15.2 us
    all_to_all x1, waiting for transfers between devices, shards(): lax.all_to_all(chunks, 'seq', 0, 0, axis_index_groups=columns, tiled=True)  9.43 us
    ppermute x1, waiting for transfers between devices, shards(): lax.ppermute(molecule_kv, 'section', [((i - 1) % sections, i) for i in ra...  4.57 us
    dot_general x1, matrix products, shards(): jnp.dot(normed, w_query, preferred_element_type=jnp.float32)  4.22 us
    ppermute x1, starting transfers between devices, shards(): lax.ppermute(molecule_kv, 'section', [((i - 1) % sections, i) for i in ra...  1.91 us
    pallas_call x1, Pallas kernels, shards(): pl.pallas_call(attend_kernel, out_shape=jax.ShapeDtypeStruct((chars, HQ),...  1.51 us
    reduce_sum x1, other arithmetic, norm_rows(): jnp.mean(values * values, axis=-1, keepdims=True) + 1e-06  1.23 us
  transfers between devices with their start and end apart: 2, of which 2 were waited for; matrix products, arithmetic and copies ran while one was open for 11% of the time, Pallas kernels for 0%

profile of v2, /device:TPU:32, one launch (start us, length us, event | category | flops | bytes accessed | tf_op | source)
XLA Modules:
  0.0 56.8 jit_solution(13090747943423857210)
XLA Ops:
  0.0 1.9 %collective-permute-start = (bf16[1,16,4096]{2,1,0:T(8,128)(2,1)}, bf16[1,16,4096]{2,1,0:T(8,128)(2,1)S(1)}, u32[]{:S(2)}, u32[]{:S(2)}) collective-permute-start(bf16[1,16,4096]{2,1,0:T(8,128)(2,1)} %param.6), channel_id=1, source_target_pairs={{384,0},{0,128},{128,256},{256,384},{385,1},{1,129},{129,257},{257... | collective-permute-start | bytes 393224 | tf_op jit(solution)/shard_map/ppermute | solution.py:104
  1.9 4.6 %collective-permute-done = bf16[1,16,4096]{2,1,0:T(8,128)(2,1)S(1)} collective-permute-done((bf16[1,16,4096]{2,1,0:T(8,128)(2,1)}, bf16[1,16,4096]{2,1,0:T(8,128)(2,1)S(1)}, u32[]{:S(2)}, u32[]{:S(2)}) %collective-permute-start) | collective-permute-done | bytes 131104 | tf_op jit(solution)/shard_map/ppermute | solution.py:104
  6.5 0.7 %shard_map.55 = bf16[16,16,384]{2,1,0:T(8,128)(2,1)} custom-call(bf16[16,4096]{1,0:T(8,128)(2,1)S(1)} %bitcast.18), custom_call_target="tpu_custom_call" | custom-call | tf_op jit(solution)/shard_map/pallas_call | solution.py:115
  7.2 15.2 %all-to-all-start = ((bf16[16,16,384]{2,1,0:T(8,128)(2,1)}), bf16[16,16,384]{2,1,0:T(8,128)(2,1)S(1)}, u32[]{:S(2)}, u32[]{:S(2)}) async-start(bf16[16,16,384]{2,1,0:T(8,128)(2,1)} %shard_map.55), calls=%async_computation | async-start | bytes 393216 | tf_op jit(solution)/shard_map/all_to_all | solution.py:122
  22.4 0.7 %fusion.8 = (f32[1024]{0:T(1024)S(1)}, f32[1024]{0:T(1024)S(1)}) fusion(f32[2048]{0:T(1024)} %param.8), kind=kLoop, calls=%fused_computation.13 | loop fusion | bytes 16384 | tf_op jit(solution)/shard_map/slice | solution.py:113
  23.1 0.1 mul.40
  23.2 1.2 %fusion = f32[128]{0:T(128)S(1)} fusion(bf16[1,128,2048]{2,1,0:T(8,128)(2,1)} %param.5), kind=kLoop, calls=%fused_computation.3 | loop fusion | flops 786304 | bytes 524800 | tf_op jit(solution)/shard_map/reduce_sum | solution.py:24
  24.4 4.2 %fusion.4 = (f32[16,128]{1,0:T(8,128)S(1)}, bf16[128,1024]{0,1:T(8,128)(2,1)S(1)}) fusion(f32[16,64]{1,0:T(8,128)S(1)} %mul.40, bf16[2048,1024]{1,0:T(8,128)(2,1)} %param.9, bf16[1,128,2048]{2,1,0:T(8,128)(2,1)} %param.5, f32[2048]{0:T(1024)} %param.7, f32[128]{0:T(128)S(1)} %add_rsqrt_fusion), kind=kOutput, calls=%fused_computation.7 | convolution fusion | flops 538441728 | bytes 5001728 | tf_op jit(solution)/shard_map/dot_general | solution.py:108
  28.6 9.4 %all-to-all-done.in_ref = bf16[16,16,384]{2,1,0:T(8,128)(2,1)S(1)} async-done(((bf16[16,16,384]{2,1,0:T(8,128)(2,1)}), bf16[16,16,384]{2,1,0:T(8,128)(2,1)S(1)}, u32[]{:S(2)}, u32[]{:S(2)}) %all-to-all-start) | async-done | bytes 196640 | tf_op jit(solution)/shard_map/all_to_all | solution.py:122
  38.1 0.2 broadcast_in_dim.4.value_ref
  38.3 0.3 shard_map.56
  38.5 16.7 %all_to_all.10.kv_ref = bf16[8,256,128]{2,1,0:T(8,128)(2,1)S(1)} all-to-all(bf16[8,256,128]{2,1,0:T(8,128)(2,1)S(1)} %shard_map.56), channel_id=1, replica_groups={{0,1,2,3,4,5,6,7},{8,9,10,11,12,13,14,15},{16,17,18,19,20,21,22,23},{24..., dimensions={0} | all-to-all | bytes 1048576 | tf_op jit(solution)/shard_map/all_to_all | solution.py:131
  55.3 1.5 %shard_map.57 = bf16[128,1024]{1,0:T(8,128)(2,1)} custom-call(bf16[1024,128]{1,0:T(8,128)(2,1)S(1)} %bitcast.17, bf16[8,256,128]{2,1,0:T(8,128)(2,1)S(1)} %all_to_all.10.kv_ref, f32[16,128]{1,0:T(8,128)S(1)} %broadcast_multiply_fusion.sink_ref, f32[1024,128]{1,0:T(8,128)S(1)} %broadcast_in_dim.4.value_ref), custom_call_target="tpu_custom_call" | custom-call | tf_op jit(solution)/shard_map/pallas_call | solution.py:132
  (2 shorter events, 0.0 us)
Async XLA Ops:
  0.0 6.5 %collective-permute-start = (bf16[1,16,4096]{2,1,0:T(8,128)(2,1)}, bf16[1,16,4096]{2,1,0:T(8,128)(2,1)S(1)}, u32[]{:S(2)}, u32[]{:S(2)}) collective-permute-start(bf16[1,16,4096]{2,1,0:T(8,128)(2,1)} %param.6), channel_id=1, source_target_pairs={{384,0},{0,128},{128,256},{256,384},{385,1},{1,129},{129,257},{257... | collective-permute-start | bytes 393224 | tf_op jit(solution)/shard_map/ppermute | solution.py:104
  7.2 30.9 %all-to-all-start = ((bf16[16,16,384]{2,1,0:T(8,128)(2,1)}), bf16[16,16,384]{2,1,0:T(8,128)(2,1)S(1)}, u32[]{:S(2)}, u32[]{:S(2)}) async-start(bf16[16,16,384]{2,1,0:T(8,128)(2,1)} %shard_map.55), calls=%async_computation | async-start | bytes 393216 | tf_op jit(solution)/shard_map/all_to_all | solution.py:122

commit v3 on v2

--- a/solution.py
+++ b/solution.py
@@ -14,9 +14,16 @@
 HQ = 1024
 LANES = 128
 PLANE = 8
+PLACES = (5, 4, 7, 6, 1, 0, 3, 2)
 ROWS = 16
 VMEM = pl.BlockSpec(memory_space=pltpu.VMEM)
 SMALL = pltpu.CompilerParams(vmem_limit_bytes=16 * 1024 * 1024)
+
+
+def plane_order(planes):
+    bits = planes.bit_length() - 1
+    turned = [int(format(i, "b").zfill(bits)[::-1], 2) for i in range(planes)]
+    return tuple((i + planes * 11 // 16) % planes for i in turned)
 
 
 def norm_rows(rows, gain):
@@ -25,11 +32,11 @@
     return (values * inverse * gain).astype(jnp.bfloat16)
 
 
-def spread_kernel(kv_ref, out_ref):
+def spread_kernel(order, kv_ref, out_ref):
     planes, _, wide = out_ref.shape
     step = kv_ref.shape[1] // planes
-    for c in range(planes):
-        first = c * step - (wide - step)
+    for c, plane in enumerate(order):
+        first = plane * step - (wide - step)
         if first < 0:
             out_ref[c, :, : wide - step] = jnp.zeros((ROWS, wide - step), jnp.bfloat16)
             out_ref[c, :, wide - step :] = kv_ref[:, :step]
@@ -40,12 +47,12 @@
 def window_kernel(in_ref, out_ref):
     rows = in_ref.shape[0] * in_ref.shape[1]
     data = in_ref[...].reshape(rows, in_ref.shape[2])
-    for w in range(PLANE):
+    for j, w in enumerate(PLACES):
         first = 32 * w + 32
-        out_ref[w] = data[:, first : first + LANES]
+        out_ref[j] = data[:, first : first + LANES]
 
 
-def attend_kernel(q_ref, kv_ref, sink_ref, value_ref, out_ref):
+def attend_kernel(order, q_ref, kv_ref, sink_ref, value_ref, out_ref):
     chars = q_ref.shape[1]
     block = lax.axis_index("seq")
     char = lax.broadcasted_iota(jnp.int32, (LANES, chars), 1)
@@ -55,8 +62,9 @@
     hidden = jnp.where(visible, jnp.float32(0.0), jnp.float32(-1e30))
     zero = jnp.zeros((HD, chars), jnp.bfloat16)
 
-    def pair(first):
-        return jnp.concatenate([kv_ref[w, first : first + ROWS, :] for w in range(PLANE)], axis=0)
+    def pair(plane):
+        first = order.index(plane) * ROWS
+        return jnp.concatenate([kv_ref[PLACES.index(w), first : first + ROWS, :] for w in range(PLANE)], axis=0)
 
     for m in range(NH // 2):
         rows = slice(m * LANES, (m + 1) * LANES)
@@ -69,7 +77,7 @@
             axis=1,
         )
         scores = lax.dot_general(
-            pair(m * ROWS), query, (((0,), (0,)), ((), ())), preferred_element_type=jnp.float32
+            pair(m), query, (((0,), (0,)), ((), ())), preferred_element_type=jnp.float32
         )
         weights, sinks = [], []
         for side in range(2):
@@ -82,7 +90,7 @@
             weights.append((expo * inverse).astype(jnp.bfloat16))
             sinks.append((sink_expo * inverse).astype(jnp.bfloat16).astype(jnp.float32))
         mixed = jnp.dot(
-            pair((m + NH // 2) * ROWS),
+            pair(m + NH // 2),
             jnp.concatenate(weights, axis=1),
             preferred_element_type=jnp.float32,
         )
@@ -97,8 +105,9 @@
     seq = lax.axis_size("seq")
     sections = lax.axis_size("section")
     planes = seq // PLANE
-    columns = [[z * PLANE + w for z in range(planes)] for w in range(PLANE)]
-    rows = [[z * PLANE + w for w in range(PLANE)] for z in range(planes)]
+    order = plane_order(planes)
+    columns = [[z * PLANE + w for z in order] for w in range(PLANE)]
+    rows = [[z * PLANE + w for w in PLACES] for z in range(planes)]
     width = molecule_kv.shape[2] // planes
 
     arrived = lax.ppermute(
@@ -113,7 +122,7 @@
     sink_value = jnp.broadcast_to(sink_kv[HQ:, None], (HQ, chars))
 
     chunks = pl.pallas_call(
-        spread_kernel,
+        functools.partial(spread_kernel, order),
         out_shape=jax.ShapeDtypeStruct((planes, ROWS, width + LANES), jnp.bfloat16),
         in_specs=[VMEM],
         out_specs=VMEM,
@@ -130,7 +139,7 @@
     )(chunks)
     keyval = lax.all_to_all(windows, "seq", 0, 0, axis_index_groups=rows, tiled=True)
     mixed = pl.pallas_call(
-        attend_kernel,
+        functools.partial(attend_kernel, order),
         out_shape=jax.ShapeDtypeStruct((chars, HQ), jnp.bfloat16),
         in_specs=[VMEM] * 4,
         out_specs=VMEM,

time: 57.1 us -> 49.6 us (0.87)
  the two profiles are of different devices: /device:TPU:32 before, /device:TPU:4 now
where the time goes in v3:
time: 49.6 us; the launch traced here: 49.3 us
  starting transfers between devices  18.1 us (36%)
  blocking collectives  12.8 us (26%)
  waiting for transfers between devices  9.5 us (19%)
  matrix products  4.22 us (9%)
  Pallas kernels  2.48 us (5%)
  other arithmetic  1.24 us (2%)
  local copies, waits for them, and re-layouts  0.96 us (2%)
    all_to_all x1, starting transfers between devices, shards(): lax.all_to_all(chunks, 'seq', 0, 0, axis_index_groups=columns, tiled=True)  16.2 us
    all_to_all x1, blocking collectives, shards(): lax.all_to_all(windows, 'seq', 0, 0, axis_index_groups=rows, tiled=True)  12.8 us
    all_to_all x1, waiting for transfers between devices, shards(): lax.all_to_all(chunks, 'seq', 0, 0, axis_index_groups=columns, tiled=True)  4.94 us
    ppermute x1, waiting for transfers between devices, shards(): lax.ppermute(molecule_kv, 'section', [((i - 1) % sections, i) for i in ra...  4.57 us
    dot_general x1, matrix products, shards(): jnp.dot(normed, w_query, preferred_element_type=jnp.float32)  4.22 us
    ppermute x1, starting transfers between devices, shards(): lax.ppermute(molecule_kv, 'section', [((i - 1) % sections, i) for i in ra...  1.91 us
    pallas_call x1, Pallas kernels, shards(): pl.pallas_call(functools.partial(attend_kernel, order), out_shape=jax.Sha...  1.51 us
    reduce_sum x1, other arithmetic, norm_rows(): jnp.mean(values * values, axis=-1, keepdims=True) + 1e-06  1.23 us
  transfers between devices with their start and end apart: 2, of which 2 were waited for; matrix products, arithmetic and copies ran while one was open for 13% of the time, Pallas kernels for 0%

profile of v3, /device:TPU:4, one launch (start us, length us, event | category | flops | bytes accessed | tf_op | source)
XLA Modules:
  0.0 49.3 jit_solution(8685890694941566230)
XLA Ops:
  0.0 1.9 %collective-permute-start = (bf16[1,16,4096]{2,1,0:T(8,128)(2,1)}, bf16[1,16,4096]{2,1,0:T(8,128)(2,1)S(1)}, u32[]{:S(2)}, u32[]{:S(2)}) collective-permute-start(bf16[1,16,4096]{2,1,0:T(8,128)(2,1)} %param.6), channel_id=1, source_target_pairs={{384,0},{0,128},{128,256},{256,384},{385,1},{1,129},{129,257},{257... | collective-permute-start | bytes 393224 | tf_op jit(solution)/shard_map/ppermute | solution.py:113
  1.9 4.6 %collective-permute-done = bf16[1,16,4096]{2,1,0:T(8,128)(2,1)S(1)} collective-permute-done((bf16[1,16,4096]{2,1,0:T(8,128)(2,1)}, bf16[1,16,4096]{2,1,0:T(8,128)(2,1)S(1)}, u32[]{:S(2)}, u32[]{:S(2)}) %collective-permute-start) | collective-permute-done | bytes 131104 | tf_op jit(solution)/shard_map/ppermute | solution.py:113
  6.5 0.7 %shard_map.55 = bf16[16,16,384]{2,1,0:T(8,128)(2,1)} custom-call(bf16[16,4096]{1,0:T(8,128)(2,1)S(1)} %bitcast.18), custom_call_target="tpu_custom_call" | custom-call | tf_op jit(solution)/shard_map/pallas_call | solution.py:124
  7.2 16.2 %all-to-all-start = ((bf16[16,16,384]{2,1,0:T(8,128)(2,1)}), bf16[16,16,384]{2,1,0:T(8,128)(2,1)S(1)}, u32[]{:S(2)}, u32[]{:S(2)}) async-start(bf16[16,16,384]{2,1,0:T(8,128)(2,1)} %shard_map.55), calls=%async_computation | async-start | bytes 393216 | tf_op jit(solution)/shard_map/all_to_all | solution.py:131
  23.3 0.7 %fusion.8 = (f32[1024]{0:T(1024)S(1)}, f32[1024]{0:T(1024)S(1)}) fusion(f32[2048]{0:T(1024)} %param.8), kind=kLoop, calls=%fused_computation.13 | loop fusion | bytes 16384 | tf_op jit(solution)/shard_map/slice | solution.py:122
  24.0 0.1 mul.40
  24.1 1.2 %fusion = f32[128]{0:T(128)S(1)} fusion(bf16[1,128,2048]{2,1,0:T(8,128)(2,1)} %param.5), kind=kLoop, calls=%fused_computation.3 | loop fusion | flops 786304 | bytes 524800 | tf_op jit(solution)/shard_map/reduce_sum | solution.py:31
  25.4 4.2 %fusion.4 = (f32[16,128]{1,0:T(8,128)S(1)}, bf16[128,1024]{0,1:T(8,128)(2,1)S(1)}) fusion(f32[16,64]{1,0:T(8,128)S(1)} %mul.40, bf16[2048,1024]{1,0:T(8,128)(2,1)} %param.9, bf16[1,128,2048]{2,1,0:T(8,128)(2,1)} %param.5, f32[2048]{0:T(1024)} %param.7, f32[128]{0:T(128)S(1)} %add_rsqrt_fusion), kind=kOutput, calls=%fused_computation.7 | convolution fusion | flops 538441728 | bytes 5001728 | tf_op jit(solution)/shard_map/dot_general | solution.py:117
  29.6 4.9 %all-to-all-done.in_ref = bf16[16,16,384]{2,1,0:T(8,128)(2,1)S(1)} async-done(((bf16[16,16,384]{2,1,0:T(8,128)(2,1)}), bf16[16,16,384]{2,1,0:T(8,128)(2,1)S(1)}, u32[]{:S(2)}, u32[]{:S(2)}) %all-to-all-start) | async-done | bytes 196640 | tf_op jit(solution)/shard_map/all_to_all | solution.py:131
  34.5 0.2 broadcast_in_dim.4.value_ref
  34.7 0.3 shard_map.56
  35.0 12.8 %all_to_all.10.kv_ref = bf16[8,256,128]{2,1,0:T(8,128)(2,1)S(1)} all-to-all(bf16[8,256,128]{2,1,0:T(8,128)(2,1)S(1)} %shard_map.56), channel_id=1, replica_groups={{5,4,7,6,1,0,3,2},{13,12,15,14,9,8,11,10},{21,20,23,22,17,16,19,18},{29..., dimensions={0} | all-to-all | bytes 1048576 | tf_op jit(solution)/shard_map/all_to_all | solution.py:140
  47.8 1.5 %shard_map.57 = bf16[128,1024]{1,0:T(8,128)(2,1)} custom-call(bf16[1024,128]{1,0:T(8,128)(2,1)S(1)} %bitcast.17, bf16[8,256,128]{2,1,0:T(8,128)(2,1)S(1)} %all_to_all.10.kv_ref, f32[16,128]{1,0:T(8,128)S(1)} %broadcast_multiply_fusion.sink_ref, f32[1024,128]{1,0:T(8,128)S(1)} %broadcast_in_dim.4.value_ref), custom_call_target="tpu_custom_call" | custom-call | tf_op jit(solution)/shard_map/pallas_call | solution.py:141
  (2 shorter events, 0.0 us)
Async XLA Ops:
  0.0 6.5 %collective-permute-start = (bf16[1,16,4096]{2,1,0:T(8,128)(2,1)}, bf16[1,16,4096]{2,1,0:T(8,128)(2,1)S(1)}, u32[]{:S(2)}, u32[]{:S(2)}) collective-permute-start(bf16[1,16,4096]{2,1,0:T(8,128)(2,1)} %param.6), channel_id=1, source_target_pairs={{384,0},{0,128},{128,256},{256,384},{385,1},{1,129},{129,257},{257... | collective-permute-start | bytes 393224 | tf_op jit(solution)/shard_map/ppermute | solution.py:113
  7.2 27.3 %all-to-all-start = ((bf16[16,16,384]{2,1,0:T(8,128)(2,1)}), bf16[16,16,384]{2,1,0:T(8,128)(2,1)S(1)}, u32[]{:S(2)}, u32[]{:S(2)}) async-start(bf16[16,16,384]{2,1,0:T(8,128)(2,1)} %shard_map.55), calls=%async_computation | async-start | bytes 393216 | tf_op jit(solution)/shard_map/all_to_all | solution.py:131

commit v4 on v3

--- a/solution.py
+++ b/solution.py
@@ -14,16 +14,18 @@
 HQ = 1024
 LANES = 128
 PLANE = 8
-PLACES = (5, 4, 7, 6, 1, 0, 3, 2)
+FOLD = 2
+PLANE_PLACES = (5, 4, 7, 6, 1, 0, 3, 2)
+PLACES = tuple(p for w in PLANE_PLACES for p in (PLANE + w, w))
 ROWS = 16
 VMEM = pl.BlockSpec(memory_space=pltpu.VMEM)
 SMALL = pltpu.CompilerParams(vmem_limit_bytes=16 * 1024 * 1024)
 
 
-def plane_order(planes):
-    bits = planes.bit_length() - 1
-    turned = [int(format(i, "b").zfill(bits)[::-1], 2) for i in range(planes)]
-    return tuple((i + planes * 11 // 16) % planes for i in turned)
+def part_order(parts):
+    bits = parts.bit_length() - 1
+    turned = [int(format(i, "b").zfill(bits)[::-1], 2) for i in range(parts)]
+    return tuple((i + parts * 5 // 8) % parts for i in turned)
 
 
 def norm_rows(rows, gain):
@@ -33,10 +35,10 @@
 
 
 def spread_kernel(order, kv_ref, out_ref):
-    planes, _, wide = out_ref.shape
-    step = kv_ref.shape[1] // planes
-    for c, plane in enumerate(order):
-        first = plane * step - (wide - step)
+    parts, _, wide = out_ref.shape
+    step = kv_ref.shape[1] // parts
+    for c, part in enumerate(order):
+        first = part * step - (wide - step)
         if first < 0:
             out_ref[c, :, : wide - step] = jnp.zeros((ROWS, wide - step), jnp.bfloat16)
             out_ref[c, :, wide - step :] = kv_ref[:, :step]
@@ -63,8 +65,9 @@
     zero = jnp.zeros((HD, chars), jnp.bfloat16)
 
     def pair(plane):
-        first = order.index(plane) * ROWS
-        return jnp.concatenate([kv_ref[PLACES.index(w), first : first + ROWS, :] for w in range(PLANE)], axis=0)
+        first = order.index(plane // FOLD) * ROWS
+        slots = [PLACES.index(plane % FOLD * PLANE + w) for w in range(PLANE)]
+        return jnp.concatenate([kv_ref[s, first : first + ROWS, :] for s in slots], axis=0)
 
     for m in range(NH // 2):
         rows = slice(m * LANES, (m + 1) * LANES)
@@ -105,10 +108,12 @@
     seq = lax.axis_size("seq")
     sections = lax.axis_size("section")
     planes = seq // PLANE
-    order = plane_order(planes)
-    columns = [[z * PLANE + w for z in order] for w in range(PLANE)]
-    rows = [[z * PLANE + w for w in PLACES] for z in range(planes)]
-    width = molecule_kv.shape[2] // planes
+    order = part_order(planes // FOLD)
+    parts = planes // FOLD
+    stride = FOLD * PLANE
+    columns = [[z * stride + w for z in order] for w in range(stride)]
+    rows = [[z * stride + w for w in PLACES] for z in range(parts)]
+    width = molecule_kv.shape[2] // parts
 
     arrived = lax.ppermute(
         molecule_kv, "section", [((i - 1) % sections, i) for i in range(sections)]
@@ -123,7 +128,7 @@
 
     chunks = pl.pallas_call(
         functools.partial(spread_kernel, order),
-        out_shape=jax.ShapeDtypeStruct((planes, ROWS, width + LANES), jnp.bfloat16),
+        out_shape=jax.ShapeDtypeStruct((parts, ROWS, width + LANES), jnp.bfloat16),
         in_specs=[VMEM],
         out_specs=VMEM,
         compiler_params=SMALL,
@@ -132,7 +137,7 @@
     chunks, turned, sink, sink_value = lax.optimization_barrier((chunks, turned, sink, sink_value))
     windows = pl.pallas_call(
         window_kernel,
-        out_shape=jax.ShapeDtypeStruct((PLANE, planes * ROWS, LANES), jnp.bfloat16),
+        out_shape=jax.ShapeDtypeStruct((stride, parts * ROWS, LANES), jnp.bfloat16),
         in_specs=[VMEM],
         out_specs=VMEM,
         compiler_params=SMALL,

time: 49.6 us -> 48.4 us (0.976)
  the two profiles are of different devices: /device:TPU:4 before, /device:TPU:16 now
where the time goes in v4:
time: 48.4 us; the launch traced here: 48.1 us
  starting transfers between devices  18.5 us (38%)
  blocking collectives  14.1 us (29%)
  waiting for transfers between devices  6.6 us (14%)
  matrix products  4.22 us (9%)
  Pallas kernels  2.42 us (5%)
  other arithmetic  1.24 us (3%)
  local copies, waits for them, and re-layouts  0.97 us (2%)
    all_to_all x1, starting transfers between devices, shards(): lax.all_to_all(chunks, 'seq', 0, 0, axis_index_groups=columns, tiled=True)  16.6 us
    all_to_all x1, blocking collectives, shards(): lax.all_to_all(windows, 'seq', 0, 0, axis_index_groups=rows, tiled=True)  14.1 us
    dot_general x1, matrix products, shards(): jnp.dot(normed, w_query, preferred_element_type=jnp.float32)  4.22 us
    ppermute x1, waiting for transfers between devices, shards(): lax.ppermute(molecule_kv, 'section', [((i - 1) % sections, i) for i in ra...  3.79 us
    all_to_all x1, waiting for transfers between devices, shards(): lax.all_to_all(chunks, 'seq', 0, 0, axis_index_groups=columns, tiled=True)  2.81 us
    ppermute x1, starting transfers between devices, shards(): lax.ppermute(molecule_kv, 'section', [((i - 1) % sections, i) for i in ra...  1.91 us
    pallas_call x1, Pallas kernels, shards(): pl.pallas_call(functools.partial(attend_kernel, order), out_shape=jax.Sha...  1.52 us
    reduce_sum x1, other arithmetic, norm_rows(): jnp.mean(values * values, axis=-1, keepdims=True) + 1e-06  1.23 us
  transfers between devices with their start and end apart: 2, of which 2 were waited for; matrix products, arithmetic and copies ran while one was open for 13% of the time, Pallas kernels for 0%

profile of v4, /device:TPU:16, one launch (start us, length us, event | category | flops | bytes accessed | tf_op | source)
XLA Modules:
  0.0 48.1 jit_solution(1641063562951390403)
XLA Ops:
  0.0 1.9 %collective-permute-start = (bf16[1,16,4096]{2,1,0:T(8,128)(2,1)}, bf16[1,16,4096]{2,1,0:T(8,128)(2,1)S(1)}, u32[]{:S(2)}, u32[]{:S(2)}) collective-permute-start(bf16[1,16,4096]{2,1,0:T(8,128)(2,1)} %param.6), channel_id=1, source_target_pairs={{384,0},{0,128},{128,256},{256,384},{385,1},{1,129},{129,257},{257... | collective-permute-start | bytes 393224 | tf_op jit(solution)/shard_map/ppermute | solution.py:118
  1.9 0.7 %fusion.8 = (f32[1024]{0:T(1024)S(1)}, f32[1024]{0:T(1024)S(1)}) fusion(f32[2048]{0:T(1024)} %param.8), kind=kLoop, calls=%fused_computation.13 | loop fusion | bytes 16384 | tf_op jit(solution)/shard_map/slice | solution.py:127
  2.6 0.1 mul.40
  2.7 3.8 %collective-permute-done = bf16[1,16,4096]{2,1,0:T(8,128)(2,1)S(1)} collective-permute-done((bf16[1,16,4096]{2,1,0:T(8,128)(2,1)}, bf16[1,16,4096]{2,1,0:T(8,128)(2,1)S(1)}, u32[]{:S(2)}, u32[]{:S(2)}) %collective-permute-start) | collective-permute-done | bytes 131104 | tf_op jit(solution)/shard_map/ppermute | solution.py:118
  6.5 0.7 %shard_map.55 = bf16[8,16,640]{2,1,0:T(8,128)(2,1)} custom-call(bf16[16,4096]{1,0:T(8,128)(2,1)S(1)} %bitcast.18), custom_call_target="tpu_custom_call" | custom-call | tf_op jit(solution)/shard_map/pallas_call | solution.py:129
  7.2 16.6 %all-to-all-start = ((bf16[8,16,640]{2,1,0:T(8,128)(2,1)}), bf16[8,16,640]{2,1,0:T(8,128)(2,1)S(1)}, u32[]{:S(2)}, u32[]{:S(2)}) async-start(bf16[8,16,640]{2,1,0:T(8,128)(2,1)} %shard_map.55), calls=%async_computation | async-start | bytes 327680 | tf_op jit(solution)/shard_map/all_to_all | solution.py:136
  23.7 1.2 %fusion = f32[128]{0:T(128)S(1)} fusion(bf16[1,128,2048]{2,1,0:T(8,128)(2,1)} %param.5), kind=kLoop, calls=%fused_computation.3 | loop fusion | flops 786304 | bytes 524800 | tf_op jit(solution)/shard_map/reduce_sum | solution.py:33
  25.0 4.2 %fusion.4 = (f32[16,128]{1,0:T(8,128)S(1)}, bf16[128,1024]{0,1:T(8,128)(2,1)S(1)}) fusion(f32[16,64]{1,0:T(8,128)S(1)} %mul.40, bf16[2048,1024]{1,0:T(8,128)(2,1)} %param.9, bf16[1,128,2048]{2,1,0:T(8,128)(2,1)} %param.5, f32[2048]{0:T(1024)} %param.7, f32[128]{0:T(128)S(1)} %add_rsqrt_fusion), kind=kOutput, calls=%fused_computation.7 | convolution fusion | flops 538441728 | bytes 5001728 | tf_op jit(solution)/shard_map/dot_general | solution.py:122
  29.2 2.8 %all-to-all-done.in_ref = bf16[8,16,640]{2,1,0:T(8,128)(2,1)S(1)} async-done(((bf16[8,16,640]{2,1,0:T(8,128)(2,1)}), bf16[8,16,640]{2,1,0:T(8,128)(2,1)S(1)}, u32[]{:S(2)}, u32[]{:S(2)}) %all-to-all-start) | async-done | bytes 163872 | tf_op jit(solution)/shard_map/all_to_all | solution.py:136
  32.0 0.2 broadcast_in_dim.4.value_ref
  32.2 0.2 shard_map.56
  32.5 14.1 %all_to_all.10.kv_ref = bf16[16,128,128]{2,1,0:T(8,128)(2,1)S(1)} all-to-all(bf16[16,128,128]{2,1,0:T(8,128)(2,1)S(1)} %shard_map.56), channel_id=1, replica_groups={{13,5,12,4,15,7,14,6,9,1,8,0,11,3,10,2},{29,21,28,20,31,23,30,22,25,17,..., dimensions={0} | all-to-all | bytes 1048576 | tf_op jit(solution)/shard_map/all_to_all | solution.py:145
  46.5 1.5 %shard_map.57 = bf16[128,1024]{1,0:T(8,128)(2,1)} custom-call(bf16[1024,128]{1,0:T(8,128)(2,1)S(1)} %bitcast.17, bf16[16,128,128]{2,1,0:T(8,128)(2,1)S(1)} %all_to_all.10.kv_ref, f32[16,128]{1,0:T(8,128)S(1)} %broadcast_multiply_fusion.sink_ref, f32[1024,128]{1,0:T(8,128)S(1)} %broadcast_in_dim.4.value_ref), custom_call_target="tpu_custom_call" | custom-call | tf_op jit(solution)/shard_map/pallas_call | solution.py:146
  (2 shorter events, 0.0 us)
Async XLA Ops:
  0.0 6.5 %collective-permute-start = (bf16[1,16,4096]{2,1,0:T(8,128)(2,1)}, bf16[1,16,4096]{2,1,0:T(8,128)(2,1)S(1)}, u32[]{:S(2)}, u32[]{:S(2)}) collective-permute-start(bf16[1,16,4096]{2,1,0:T(8,128)(2,1)} %param.6), channel_id=1, source_target_pairs={{384,0},{0,128},{128,256},{256,384},{385,1},{1,129},{129,257},{257... | collective-permute-start | bytes 393224 | tf_op jit(solution)/shard_map/ppermute | solution.py:118
  7.2 24.9 %all-to-all-start = ((bf16[8,16,640]{2,1,0:T(8,128)(2,1)}), bf16[8,16,640]{2,1,0:T(8,128)(2,1)S(1)}, u32[]{:S(2)}, u32[]{:S(2)}) async-start(bf16[8,16,640]{2,1,0:T(8,128)(2,1)} %shard_map.55), calls=%async_computation | async-start | bytes 327680 | tf_op jit(solution)/shard_map/all_to_all | solution.py:136

commit v5 on v4

--- a/solution.py
+++ b/solution.py
@@ -15,8 +15,7 @@
 LANES = 128
 PLANE = 8
 FOLD = 2
-PLANE_PLACES = (5, 4, 7, 6, 1, 0, 3, 2)
-PLACES = tuple(p for w in PLANE_PLACES for p in (PLANE + w, w))
+PLACES = (13, 5, 15, 7, 12, 4, 14, 6, 11, 3, 9, 1, 10, 2, 8, 0)
 ROWS = 16
 VMEM = pl.BlockSpec(memory_space=pltpu.VMEM)
 SMALL = pltpu.CompilerParams(vmem_limit_bytes=16 * 1024 * 1024)
@@ -26,12 +25,6 @@
     bits = parts.bit_length() - 1
     turned = [int(format(i, "b").zfill(bits)[::-1], 2) for i in range(parts)]
     return tuple((i + parts * 5 // 8) % parts for i in turned)
-
-
-def norm_rows(rows, gain):
-    values = rows.astype(jnp.float32)
-    inverse = lax.rsqrt(jnp.mean(values * values, axis=-1, keepdims=True) + 1e-06)
-    return (values * inverse * gain).astype(jnp.bfloat16)
 
 
 def spread_kernel(order, kv_ref, out_ref):
@@ -118,13 +111,16 @@
     arrived = lax.ppermute(
         molecule_kv, "section", [((i - 1) % sections, i) for i in range(sections)]
     )[0]
-    normed = norm_rows(skip_rows[0], norm_gain)
+    values = skip_rows[0].astype(jnp.float32)
+    inverse = lax.rsqrt(jnp.mean(values * values, axis=-1, keepdims=True) + 1e-06)
+    chars = values.shape[0]
+    sink_value = jnp.broadcast_to(sink_kv[HQ:, None], (HQ, chars))
+    arrived, inverse, sink_value = lax.optimization_barrier((arrived, inverse, sink_value))
+    normed = (values * inverse * norm_gain).astype(jnp.bfloat16)
     query = jnp.dot(normed, w_query, preferred_element_type=jnp.float32).astype(jnp.bfloat16)
-    chars = query.shape[0]
     turned = query.T
     sink = turned.astype(jnp.float32).reshape(NH, HD, chars) * sink_kv[:HQ].reshape(NH, HD, 1)
     sink = jnp.sum(sink, axis=1) * 0.125
-    sink_value = jnp.broadcast_to(sink_kv[HQ:, None], (HQ, chars))
 
     chunks = pl.pallas_call(
         functools.partial(spread_kernel, order),
@@ -134,7 +130,7 @@
         compiler_params=SMALL,
     )(arrived)
     chunks = lax.all_to_all(chunks, "seq", 0, 0, axis_index_groups=columns, tiled=True)
-    chunks, turned, sink, sink_value = lax.optimization_barrier((chunks, turned, sink, sink_value))
+    chunks, turned, sink = lax.optimization_barrier((chunks, turned, sink))
     windows = pl.pallas_call(
         window_kernel,
         out_shape=jax.ShapeDtypeStruct((stride, parts * ROWS, LANES), jnp.bfloat16),

time: 48.4 us -> 48.3 us (level)
  the two profiles are of different devices: /device:TPU:16 before, /device:TPU:2 now
where the time goes in v5:
time: 48.3 us; the launch traced here: 48 us
  starting transfers between devices  18.5 us (38%)
  blocking collectives  13.7 us (28%)
  waiting for transfers between devices  6.9 us (14%)
  matrix products  4.21 us (9%)
  Pallas kernels  2.42 us (5%)
  other arithmetic  1.24 us (3%)
  local copies, waits for them, and re-layouts  0.96 us (2%)
    all_to_all x1, starting transfers between devices, shards(): lax.all_to_all(chunks, 'seq', 0, 0, axis_index_groups=columns, tiled=True)  16.6 us
    all_to_all x1, blocking collectives, shards(): lax.all_to_all(windows, 'seq', 0, 0, axis_index_groups=rows, tiled=True)  13.7 us
    all_to_all x1, waiting for transfers between devices, shards(): lax.all_to_all(chunks, 'seq', 0, 0, axis_index_groups=columns, tiled=True)  4.27 us
    dot_general x1, matrix products, shards(): jnp.dot(normed, w_query, preferred_element_type=jnp.float32)  4.21 us
    ppermute x1, waiting for transfers between devices, shards(): lax.ppermute(molecule_kv, 'section', [((i - 1) % sections, i) for i in ra...  2.63 us
    ppermute x1, starting transfers between devices, shards(): lax.ppermute(molecule_kv, 'section', [((i - 1) % sections, i) for i in ra...  1.91 us
    pallas_call x1, Pallas kernels, shards(): pl.pallas_call(functools.partial(attend_kernel, order), out_shape=jax.Sha...  1.52 us
    reduce_sum x1, other arithmetic, shards(): jnp.mean(values * values, axis=-1, keepdims=True) + 1e-06  1.23 us
  transfers between devices with their start and end apart: 2, of which 2 were waited for; matrix products, arithmetic and copies ran while one was open for 13% of the time, Pallas kernels for 0%

profile of v5, /device:TPU:2, one launch (start us, length us, event | category | flops | bytes accessed | tf_op | source)
XLA Modules:
  0.0 48.0 jit_solution(7789570330421573766)
XLA Ops:
  0.0 1.9 %collective-permute-start = (bf16[1,16,4096]{2,1,0:T(8,128)(2,1)}, bf16[1,16,4096]{2,1,0:T(8,128)(2,1)S(1)}, u32[]{:S(2)}, u32[]{:S(2)}) collective-permute-start(bf16[1,16,4096]{2,1,0:T(8,128)(2,1)} %param.6), channel_id=1, source_target_pairs={{384,0},{0,128},{128,256},{256,384},{385,1},{1,129},{129,257},{257... | collective-permute-start | bytes 393224 | tf_op jit(solution)/shard_map/ppermute | solution.py:111
  1.9 1.2 %fusion = f32[128]{0:T(128)S(1)} fusion(bf16[1,128,2048]{2,1,0:T(8,128)(2,1)} %param.5), kind=kLoop, calls=%fused_computation.3 | loop fusion | flops 786304 | bytes 524800 | tf_op jit(solution)/shard_map/reduce_sum | solution.py:115
  3.1 0.7 %fusion.8 = (f32[1024]{0:T(1024)S(1)}, f32[1024]{0:T(1024)S(1)}) fusion(f32[2048]{0:T(1024)} %param.8), kind=kLoop, calls=%fused_computation.13 | loop fusion | bytes 16384 | tf_op jit(solution)/shard_map/slice | solution.py:122
  3.9 2.6 %collective-permute-done = bf16[1,16,4096]{2,1,0:T(8,128)(2,1)S(1)} collective-permute-done((bf16[1,16,4096]{2,1,0:T(8,128)(2,1)}, bf16[1,16,4096]{2,1,0:T(8,128)(2,1)S(1)}, u32[]{:S(2)}, u32[]{:S(2)}) %collective-permute-start) | collective-permute-done | bytes 131104 | tf_op jit(solution)/shard_map/ppermute | solution.py:111
  6.5 0.2 broadcast_in_dim.4.value_ref
  6.7 0.7 %shard_map.55 = bf16[8,16,640]{2,1,0:T(8,128)(2,1)} custom-call(bf16[16,4096]{1,0:T(8,128)(2,1)S(1)} %bitcast.21), custom_call_target="tpu_custom_call" | custom-call | tf_op jit(solution)/shard_map/pallas_call | solution.py:125
  7.4 16.6 %all-to-all-start = ((bf16[8,16,640]{2,1,0:T(8,128)(2,1)}), bf16[8,16,640]{2,1,0:T(8,128)(2,1)S(1)}, u32[]{:S(2)}, u32[]{:S(2)}) async-start(bf16[8,16,640]{2,1,0:T(8,128)(2,1)} %shard_map.55), calls=%async_computation | async-start | bytes 327680 | tf_op jit(solution)/shard_map/all_to_all | solution.py:132
  24.0 0.1 mul.43
  24.0 4.2 %fusion.4 = (f32[16,128]{1,0:T(8,128)S(1)}, bf16[128,1024]{0,1:T(8,128)(2,1)S(1)}) fusion(f32[16,64]{1,0:T(8,128)S(1)} %mul.43, bf16[2048,1024]{1,0:T(8,128)(2,1)} %param.9, bf16[1,128,2048]{2,1,0:T(8,128)(2,1)} %param.5, f32[2048]{0:T(1024)} %param.7, f32[128]{0:T(128)S(1)} %bitcast.22), kind=kOutput, calls=%fused_computation.7 | convolution fusion | flops 538441728 | bytes 5001728 | tf_op jit(solution)/shard_map/dot_general | solution.py:120
  28.2 4.3 %all-to-all-done.in_ref = bf16[8,16,640]{2,1,0:T(8,128)(2,1)S(1)} async-done(((bf16[8,16,640]{2,1,0:T(8,128)(2,1)}), bf16[8,16,640]{2,1,0:T(8,128)(2,1)S(1)}, u32[]{:S(2)}, u32[]{:S(2)}) %all-to-all-start) | async-done | bytes 163872 | tf_op jit(solution)/shard_map/all_to_all | solution.py:132
  32.5 0.2 shard_map.56
  32.7 13.7 %all_to_all.10.kv_ref = bf16[16,128,128]{2,1,0:T(8,128)(2,1)S(1)} all-to-all(bf16[16,128,128]{2,1,0:T(8,128)(2,1)S(1)} %shard_map.56), channel_id=1, replica_groups={{13,5,15,7,12,4,14,6,11,3,9,1,10,2,8,0},{29,21,31,23,28,20,30,22,27,19,..., dimensions={0} | all-to-all | bytes 1048576 | tf_op jit(solution)/shard_map/all_to_all | solution.py:141
  46.4 1.5 %shard_map.57 = bf16[128,1024]{1,0:T(8,128)(2,1)} custom-call(bf16[1024,128]{1,0:T(8,128)(2,1)S(1)} %bitcast.20, bf16[16,128,128]{2,1,0:T(8,128)(2,1)S(1)} %all_to_all.10.kv_ref, f32[16,128]{1,0:T(8,128)S(1)} %broadcast_multiply_fusion.sink_ref, f32[1024,128]{1,0:T(8,128)S(1)} %broadcast_in_dim.4.value_ref), custom_call_target="tpu_custom_call" | custom-call | tf_op jit(solution)/shard_map/pallas_call | solution.py:142
  (2 shorter events, 0.0 us)
Async XLA Ops:
  0.0 6.5 %collective-permute-start = (bf16[1,16,4096]{2,1,0:T(8,128)(2,1)}, bf16[1,16,4096]{2,1,0:T(8,128)(2,1)S(1)}, u32[]{:S(2)}, u32[]{:S(2)}) collective-permute-start(bf16[1,16,4096]{2,1,0:T(8,128)(2,1)} %param.6), channel_id=1, source_target_pairs={{384,0},{0,128},{128,256},{256,384},{385,1},{1,129},{129,257},{257... | collective-permute-start | bytes 393224 | tf_op jit(solution)/shard_map/ppermute | solution.py:111
  7.4 25.2 %all-to-all-start = ((bf16[8,16,640]{2,1,0:T(8,128)(2,1)}), bf16[8,16,640]{2,1,0:T(8,128)(2,1)S(1)}, u32[]{:S(2)}, u32[]{:S(2)}) async-start(bf16[8,16,640]{2,1,0:T(8,128)(2,1)} %shard_map.55), calls=%async_computation | async-start | bytes 327680 | tf_op jit(solution)/shard_map/all_to_all | solution.py:132

commit v6 on v5

--- a/solution.py
+++ b/solution.py
@@ -18,6 +18,7 @@
 PLACES = (13, 5, 15, 7, 12, 4, 14, 6, 11, 3, 9, 1, 10, 2, 8, 0)
 ROWS = 16
 VMEM = pl.BlockSpec(memory_space=pltpu.VMEM)
+ANY = pl.BlockSpec(memory_space=pl.ANY)
 SMALL = pltpu.CompilerParams(vmem_limit_bytes=16 * 1024 * 1024)
 
 
@@ -27,16 +28,21 @@
     return tuple((i + parts * 5 // 8) % parts for i in turned)
 
 
-def spread_kernel(order, kv_ref, out_ref):
+def spread_kernel(order, kv_ref, out_ref, stage, sems):
     parts, _, wide = out_ref.shape
     step = kv_ref.shape[1] // parts
+    copies = []
     for c, part in enumerate(order):
         first = part * step - (wide - step)
         if first < 0:
-            out_ref[c, :, : wide - step] = jnp.zeros((ROWS, wide - step), jnp.bfloat16)
-            out_ref[c, :, wide - step :] = kv_ref[:, :step]
+            stage[c, :, : wide - step] = jnp.zeros((ROWS, wide - step), jnp.bfloat16)
+            stage[c, :, wide - step :] = kv_ref[:, :step]
         else:
-            out_ref[c] = kv_ref[:, first : first + wide]
+            stage[c] = kv_ref[:, first : first + wide]
+        copies.append(pltpu.make_async_copy(stage.at[c], out_ref.at[c], sems.at[c]))
+        copies[-1].start()
+    for copy in copies:
+        copy.wait()
 
 
 def window_kernel(in_ref, out_ref):
@@ -126,7 +132,11 @@
         functools.partial(spread_kernel, order),
         out_shape=jax.ShapeDtypeStruct((parts, ROWS, width + LANES), jnp.bfloat16),
         in_specs=[VMEM],
-        out_specs=VMEM,
+        out_specs=ANY,
+        scratch_shapes=[
+            pltpu.VMEM((parts, ROWS, width + LANES), jnp.bfloat16),
+            pltpu.SemaphoreType.DMA((parts,)),
+        ],
         compiler_params=SMALL,
     )(arrived)
     chunks = lax.all_to_all(chunks, "seq", 0, 0, axis_index_groups=columns, tiled=True)

time: 48.3 us -> 48.4 us (level)
  no operation moved by 1% of the time
where the time goes in v6:
time: 48.4 us; the launch traced here: 48 us
  starting transfers between devices  18.5 us (38%)
  blocking collectives  13.7 us (28%)
  waiting for transfers between devices  6.9 us (14%)
  matrix products  4.21 us (9%)
  Pallas kernels  2.46 us (5%)
  other arithmetic  1.24 us (3%)
  local copies, waits for them, and re-layouts  0.96 us (2%)
    all_to_all x1, starting transfers between devices, shards(): lax.all_to_all(chunks, 'seq', 0, 0, axis_index_groups=columns, tiled=True)  16.6 us
    all_to_all x1, blocking collectives, shards(): lax.all_to_all(windows, 'seq', 0, 0, axis_index_groups=rows, tiled=True)  13.7 us
    all_to_all x1, waiting for transfers between devices, shards(): lax.all_to_all(chunks, 'seq', 0, 0, axis_index_groups=columns, tiled=True)  4.27 us
    dot_general x1, matrix products, shards(): jnp.dot(normed, w_query, preferred_element_type=jnp.float32)  4.21 us
    ppermute x1, waiting for transfers between devices, shards(): lax.ppermute(molecule_kv, 'section', [((i - 1) % sections, i) for i in ra...  2.63 us
    ppermute x1, starting transfers between devices, shards(): lax.ppermute(molecule_kv, 'section', [((i - 1) % sections, i) for i in ra...  1.91 us
    pallas_call x1, Pallas kernels, shards(): pl.pallas_call(functools.partial(attend_kernel, order), out_shape=jax.Sha...  1.51 us
    reduce_sum x1, other arithmetic, shards(): jnp.mean(values * values, axis=-1, keepdims=True) + 1e-06  1.23 us
  transfers between devices with their start and end apart: 2, of which 2 were waited for; matrix products, arithmetic and copies ran while one was open for 13% of the time, Pallas kernels for 0%

profile of v6, /device:TPU:2, one launch (start us, length us, event | category | flops | bytes accessed | tf_op | source)
XLA Modules:
  0.0 48.0 jit_solution(10133599510383550880)
XLA Ops:
  0.0 1.9 %collective-permute-start = (bf16[1,16,4096]{2,1,0:T(8,128)(2,1)}, bf16[1,16,4096]{2,1,0:T(8,128)(2,1)S(1)}, u32[]{:S(2)}, u32[]{:S(2)}) collective-permute-start(bf16[1,16,4096]{2,1,0:T(8,128)(2,1)} %param.6), channel_id=1, source_target_pairs={{384,0},{0,128},{128,256},{256,384},{385,1},{1,129},{129,257},{257... | collective-permute-start | bytes 393224 | tf_op jit(solution)/shard_map/ppermute | solution.py:117
  1.9 1.2 %fusion = f32[128]{0:T(128)S(1)} fusion(bf16[1,128,2048]{2,1,0:T(8,128)(2,1)} %param.5), kind=kLoop, calls=%fused_computation.3 | loop fusion | flops 786304 | bytes 524800 | tf_op jit(solution)/shard_map/reduce_sum | solution.py:121
  3.1 0.7 %fusion.8 = (f32[1024]{0:T(1024)S(1)}, f32[1024]{0:T(1024)S(1)}) fusion(f32[2048]{0:T(1024)} %param.8), kind=kLoop, calls=%fused_computation.13 | loop fusion | bytes 16384 | tf_op jit(solution)/shard_map/slice | solution.py:128
  3.9 2.6 %collective-permute-done = bf16[1,16,4096]{2,1,0:T(8,128)(2,1)S(1)} collective-permute-done((bf16[1,16,4096]{2,1,0:T(8,128)(2,1)}, bf16[1,16,4096]{2,1,0:T(8,128)(2,1)S(1)}, u32[]{:S(2)}, u32[]{:S(2)}) %collective-permute-start) | collective-permute-done | bytes 131104 | tf_op jit(solution)/shard_map/ppermute | solution.py:117
  6.5 0.2 broadcast_in_dim.4.value_ref
  6.7 0.7 %shard_map.55 = bf16[8,16,640]{2,1,0:T(8,128)(2,1)} custom-call(bf16[16,4096]{1,0:T(8,128)(2,1)S(1)} %bitcast.21), custom_call_target="tpu_custom_call" | custom-call | tf_op jit(solution)/shard_map/pallas_call | solution.py:131
  7.4 16.6 %all-to-all-start = ((bf16[8,16,640]{2,1,0:T(8,128)(2,1)}), bf16[8,16,640]{2,1,0:T(8,128)(2,1)S(1)}, u32[]{:S(2)}, u32[]{:S(2)}) async-start(bf16[8,16,640]{2,1,0:T(8,128)(2,1)} %shard_map.55), calls=%async_computation | async-start | bytes 327680 | tf_op jit(solution)/shard_map/all_to_all | solution.py:142
  24.0 0.1 mul.43
  24.1 4.2 %fusion.4 = (f32[16,128]{1,0:T(8,128)S(1)}, bf16[128,1024]{0,1:T(8,128)(2,1)S(1)}) fusion(f32[16,64]{1,0:T(8,128)S(1)} %mul.43, bf16[2048,1024]{1,0:T(8,128)(2,1)} %param.9, bf16[1,128,2048]{2,1,0:T(8,128)(2,1)} %param.5, f32[2048]{0:T(1024)} %param.7, f32[128]{0:T(128)S(1)} %bitcast.22), kind=kOutput, calls=%fused_computation.7 | convolution fusion | flops 538441728 | bytes 5001728 | tf_op jit(solution)/shard_map/dot_general | solution.py:126
  28.3 4.3 %all-to-all-done.in_ref = bf16[8,16,640]{2,1,0:T(8,128)(2,1)S(1)} async-done(((bf16[8,16,640]{2,1,0:T(8,128)(2,1)}), bf16[8,16,640]{2,1,0:T(8,128)(2,1)S(1)}, u32[]{:S(2)}, u32[]{:S(2)}) %all-to-all-start) | async-done | bytes 163872 | tf_op jit(solution)/shard_map/all_to_all | solution.py:142
  32.6 0.2 shard_map.56
  32.8 13.7 %all_to_all.10.kv_ref = bf16[16,128,128]{2,1,0:T(8,128)(2,1)S(1)} all-to-all(bf16[16,128,128]{2,1,0:T(8,128)(2,1)S(1)} %shard_map.56), channel_id=1, replica_groups={{13,5,15,7,12,4,14,6,11,3,9,1,10,2,8,0},{29,21,31,23,28,20,30,22,27,19,..., dimensions={0} | all-to-all | bytes 1048576 | tf_op jit(solution)/shard_map/all_to_all | solution.py:151
  46.5 1.5 %shard_map.57 = bf16[128,1024]{1,0:T(8,128)(2,1)} custom-call(bf16[1024,128]{1,0:T(8,128)(2,1)S(1)} %bitcast.20, bf16[16,128,128]{2,1,0:T(8,128)(2,1)S(1)} %all_to_all.10.kv_ref, f32[16,128]{1,0:T(8,128)S(1)} %broadcast_multiply_fusion.sink_ref, f32[1024,128]{1,0:T(8,128)S(1)} %broadcast_in_dim.4.value_ref), custom_call_target="tpu_custom_call" | custom-call | tf_op jit(solution)/shard_map/pallas_call | solution.py:152
  (2 shorter events, 0.0 us)
Async XLA Ops:
  0.0 6.5 %collective-permute-start = (bf16[1,16,4096]{2,1,0:T(8,128)(2,1)}, bf16[1,16,4096]{2,1,0:T(8,128)(2,1)S(1)}, u32[]{:S(2)}, u32[]{:S(2)}) collective-permute-start(bf16[1,16,4096]{2,1,0:T(8,128)(2,1)} %param.6), channel_id=1, source_target_pairs={{384,0},{0,128},{128,256},{256,384},{385,1},{1,129},{129,257},{257... | collective-permute-start | bytes 393224 | tf_op jit(solution)/shard_map/ppermute | solution.py:117
  7.4 25.2 %all-to-all-start = ((bf16[8,16,640]{2,1,0:T(8,128)(2,1)}), bf16[8,16,640]{2,1,0:T(8,128)(2,1)S(1)}, u32[]{:S(2)}, u32[]{:S(2)}) async-start(bf16[8,16,640]{2,1,0:T(8,128)(2,1)} %shard_map.55), calls=%async_computation | async-start | bytes 327680 | tf_op jit(solution)/shard_map/all_to_all | solution.py:142
